TPU v7x, 32 devices: a whole 2x2x4 slice. The times are simulated.
32 devices in a mesh: ep: 8 (over z, y), dp: 4 (over x, core).
Axes of the slice: x: 2, y: 2, z: 4, core: 2. Of those that a mesh axis runs over, the one named last changes fastest.
Arguments:
- tokens: bfloat16 [512, 3584], P(('ep', 'dp')), may hold values from -6 to 6
- expert_ids: int32 [512, 8], P('ep'), may hold values from 0 to 15, all different within a row; in each aligned block of 64 rows (0 to 63, 64 to 127, ...) at most 64 rows name the same one
- gate_weights: float32 [512, 8], P('ep'), may hold values from 0.1 to 0.5
- live_counts: int32 [32], P('ep'), may hold values from 9 to 16, as said below
- w_gate: bfloat16 [16, 3584, 1024], P('ep', None, 'dp'), may hold values from -0.09375 to 0.09375
- w_up: bfloat16 [16, 3584, 1024], P('ep', None, 'dp'), may hold values from -0.09375 to 0.09375
- w_down: bfloat16 [16, 1024, 3584], P('ep', 'dp'), may hold values from -0.1875 to 0.1875
Outputs:
- moe_out: bfloat16 [512, 3584], P(('ep', 'dp'))
Inputs may be any that keep to these rules, and one draw needn't show every extreme that they name: `expert_ids`: each row names 8 different experts. Among the 64 rows of one index of ep (aligned blocks) no expert is named more than 64 times, a bound that some block reaches. `live_counts`: entry i counts the live tree tokens of the i-th block of 16 rows, which are its first ones; some entry equals 16.
All inputs are finite; a program needn't handle non-finite values.
Results may differ from a plain program's by a relative error of at most 0.012.
Values may be sent and summed in bfloat16 or wider, within the bound.
A program may use at most 128 MiB of HBM per device.

v0:
```python
import jax
import jax.numpy as jnp
from jax import lax
from jax.sharding import PartitionSpec as P


def slot_table(block_ids, block_counts, experts_all, capacity):
    row_count = block_ids.shape[0]
    top_count = block_ids.shape[1]
    per_device = row_count // block_counts.shape[0]
    positions = jnp.arange(row_count, dtype=jnp.int32)
    owners = positions // per_device
    device_ids = jnp.arange(block_counts.shape[0], dtype=jnp.int32)
    limits = jnp.sum(
        jnp.where(owners[:, None] == device_ids[None, :], block_counts[None, :], 0),
        axis=1,
        dtype=jnp.int32,
    )
    live_mask = positions % per_device < limits
    flat_ids = block_ids.reshape(-1)
    live_pairs = jnp.repeat(live_mask, top_count)
    expert_range = jnp.arange(experts_all, dtype=jnp.int32)
    one_hot = jnp.where(
        (flat_ids[:, None] == expert_range[None, :]) & live_pairs[:, None], 1, 0
    ).astype(jnp.int32)
    earlier = jnp.cumsum(one_hot, axis=0, dtype=jnp.int32) - one_hot
    slot_index = jnp.sum(earlier * one_hot, axis=1, dtype=jnp.int32)
    targets = jnp.where(live_pairs, flat_ids * capacity + slot_index, -1)
    return targets.reshape(row_count, top_count)


def expert_apply(slot_rows, gate_mat, up_mat, down_mat):
    gate_part = jnp.einsum(
        "sjnd,jdf->sjnf", slot_rows, gate_mat, preferred_element_type=jnp.float32
    )
    up_part = jnp.einsum("sjnd,jdf->sjnf", slot_rows, up_mat, preferred_element_type=jnp.float32)
    hidden_part = (jax.nn.silu(gate_part) * up_part).astype(jnp.bfloat16)
    return jnp.einsum(
        "sjnf,jfd->sjnd", hidden_part, down_mat, preferred_element_type=jnp.float32
    ).astype(jnp.bfloat16)


def body(tokens, expert_ids, gate_weights, live_counts, w_gate, w_up, w_down):
    ep_count = lax.axis_size("ep")
    local_experts = w_gate.shape[0]
    experts_all = local_experts * ep_count
    block_rows = expert_ids.shape[0]
    top_count = expert_ids.shape[1]
    model_width = tokens.shape[1]
    capacity = 2 * block_rows * top_count // experts_all
    block_tokens = lax.all_gather(tokens, "dp", axis=0, tiled=True)
    targets = slot_table(expert_ids, live_counts, experts_all, capacity)
    slot_range = jnp.arange(experts_all * capacity, dtype=jnp.int32)
    pick_matrix = jnp.sum(
        jnp.where(targets[:, :, None] == slot_range[None, None, :], 1.0, 0.0), axis=1
    ).astype(jnp.bfloat16)
    buffer = jnp.einsum(
        "rs,rd->sd", pick_matrix, block_tokens, preferred_element_type=jnp.float32
    ).astype(jnp.bfloat16)
    buffer = buffer.reshape(ep_count, local_experts, capacity, model_width)
    arrived_rows = lax.all_to_all(buffer, "ep", split_axis=0, concat_axis=0, tiled=True)
    result = expert_apply(arrived_rows, w_gate, w_up, w_down)
    returned = lax.all_to_all(result, "ep", split_axis=0, concat_axis=0, tiled=True)
    live_pairs = targets >= 0
    safe_targets = jnp.maximum(targets, 0)
    table = returned.reshape(experts_all * capacity, model_width)
    picked = jnp.take(table, safe_targets, axis=0).astype(jnp.float32)
    weights = jnp.where(live_pairs, gate_weights, 0.0)
    combined = jnp.sum(weights[:, :, None] * picked, axis=1)
    own_rows = lax.psum_scatter(
        combined.astype(jnp.bfloat16), "dp", scatter_dimension=0, tiled=True
    )
    return own_rows


def solution(mesh):
    placed = (
        P(("ep", "dp"), None),
        P("ep", None),
        P("ep", None),
        P("ep"),
        P("ep", None, "dp"),
        P("ep", None, "dp"),
        P("ep", "dp", None),
    )
    return jax.shard_map(
        body, mesh=mesh, in_specs=placed, out_specs=P(("ep", "dp"), None), check_vma=False
    )
```

profile of v0, /device:TPU:0, one launch (start us, length us, event | category | flops | bytes accessed | tf_op | source)
XLA Modules:
  0.0 424.6 jit_solution(10676828049620321621)
XLA Ops:
  6.5 0.7 select_reduce_fusion.1
  7.4 0.8 copy.38
  8.4 0.1 broadcast_in_dim.69
  8.5 1.2 reduce-window.6
  9.7 0.2 slice_reduce_fusion
  10.0 0.1 and.46
  10.1 0.1 fusion.39
  10.4 0.7 broadcast_compare_fusion
  11.2 0.7 select_reduce_fusion
  11.9 8.5 %all_gather.3 = bf16[64,3584]{1,0:T(8,128)(2,1)S(1)} all-gather(bf16[16,3584]{1,0:T(8,128)(2,1)} %param.7), channel_id=1, replica_groups=mesh['ep'=8,'dp'=4] {'dp'}, dimensions={0}, use_global_device_ids=true | all-gather | bytes 573440 | tf_op jit(solution)/shard_map/all_gather | solution.py:51
  20.4 2.1 convolution_convert_fusion.1
  22.5 167.0 %all_to_all.10 = bf16[8,2,64,3584]{3,2,1,0:T(8,128)(2,1)S(1)} all-to-all(bf16[8,2,64,3584]{3,2,1,0:T(8,128)(2,1)S(1)} %bitcast.56), channel_id=1, replica_groups=mesh['ep'=8,'dp'=4] {'ep'}, dimensions={0} | all-to-all | bytes 14680064 | tf_op jit(solution)/shard_map/all_to_all | solution.py:61
  189.4 3.0 copy-done
  192.4 2.0 fusion.8
  194.5 12.3 %fusion = bf16[8,2,64,3584]{3,2,0,1:T(8,128)(2,1)} fusion(bf16[2,256,3584]{2,1,0:T(8,128)(2,1)} %param.13, bf16[2,3584,256]{2,1,0:T(8,128)(2,1)} %param.12, bf16[8,2,64,3584]{3,2,1,0:T(8,128)(2,1)} %copy-done, f32[8,2,64,256]{3,2,0,1:T(8,128)S(1)} %fusion.8), kind=kOutput, calls=%fused_computation.4 | convolution fusion | flops 3763339264 | bytes 23068672 | tf_op jit(solution)/shard_map/sjnf,jfd->sjnd/dot_general | solution.py:38
  206.8 6.8 %copy.48 = bf16[8,2,64,3584]{3,2,1,0:T(8,128)(2,1)} copy(bf16[8,2,64,3584]{3,2,0,1:T(8,128)(2,1)} %fusion) | data formatting | bytes 14680064 | tf_op jit(solution)/shard_map/convert_element_type | solution.py:40
  213.6 5.0 %all-to-all-start.1 = ((bf16[8,2,64,3584]{3,2,1,0:T(8,128)(2,1)}), bf16[8,2,64,3584]{3,2,1,0:T(8,128)(2,1)}, u32[]{:S(2)}, u32[]{:S(2)}) async-start(bf16[8,2,64,3584]{3,2,1,0:T(8,128)(2,1)} %copy.48), calls=%async_computation.1 | async-start | bytes 14680064 | tf_op jit(solution)/shard_map/all_to_all | solution.py:63
  218.6 0.2 reduce-scatter.2.cloned.1.call-start
  218.9 0.1 reshape.75
  219.1 0.1 copy.44
  219.2 159.6 %all-to-all-done.1 = bf16[8,2,64,3584]{3,2,1,0:T(8,128)(2,1)} async-done(((bf16[8,2,64,3584]{3,2,1,0:T(8,128)(2,1)}), bf16[8,2,64,3584]{3,2,1,0:T(8,128)(2,1)}, u32[]{:S(2)}, u32[]{:S(2)}) %all-to-all-start.1) | async-done | bytes 7340064 | tf_op jit(solution)/shard_map/all_to_all | solution.py:63
  378.8 11.9 %gather_fusion = bf16[512,3584]{1,0:T(8,128)(2,1)} fusion(bf16[1024,3584]{1,0:T(8,128)(2,1)} %bitcast.11, s32[1024]{0:T(1024)S(1)} %pad_clamp_fusion), kind=kCustom, calls=%fused_computation | custom fusion | bytes 7342080 | tf_op jit(solution)/shard_map/jit(_take)/gather | solution.py:67
  390.7 7.0 %multiply_reduce_fusion = bf16[64,3584]{1,0:T(8,128)(2,1)} fusion(bf16[512,3584]{1,0:T(8,128)(2,1)} %gather_fusion, f32[64,8]{1,0:T(8,128)S(1)} %copy.43, pred[64,8]{1,0:T(8,128)(4,1)S(1)} %copy.44), kind=kLoop, calls=%fused_computation.3 | loop fusion | flops 7110656 | bytes 4131328 | tf_op jit(solution)/shard_map/reduce_sum | solution.py:69
  397.7 20.0 %reduce-scatter.2.cloned.1.call-done = bf16[16,3584]{1,0:T(8,128)(2,1)} async-done(((bf16[64,3584]{1,0:T(8,128)(2,1)}), bf16[16,3584]{1,0:T(8,128)(2,1)}) %reduce-scatter.2.cloned.1.call-update) | async-done | bytes 114704 | tf_op jit(solution)/shard_map/reduce_scatter | solution.py:70
  (25 shorter events, 0.9 us)
Async XLA Ops:
  22.4 170.0 %copy-start.2 = (bf16[2,3584,256]{2,1,0:T(8,128)(2,1)S(1)}, bf16[2,3584,256]{2,1,0:T(8,128)(2,1)}, u32[]{:S(2)}) copy-start(bf16[2,3584,256]{2,1,0:T(8,128)(2,1)} %param.11) | copy-start | bytes 11010052
  189.4 3.0 copy-start
  213.6 5.4 %copy-start.1 = (f32[64,8]{0,1:T(8,128)S(1)}, f32[64,8]{0,1:T(8,128)}, u32[]{:S(2)}) copy-start(f32[64,8]{0,1:T(8,128)} %param.9) | copy-start | bytes 6148
  213.6 165.2 %all-to-all-start.1 = ((bf16[8,2,64,3584]{3,2,1,0:T(8,128)(2,1)}), bf16[8,2,64,3584]{3,2,1,0:T(8,128)(2,1)}, u32[]{:S(2)}, u32[]{:S(2)}) async-start(bf16[8,2,64,3584]{3,2,1,0:T(8,128)(2,1)} %copy.48), calls=%async_computation.1 | async-start | bytes 14680064 | tf_op jit(solution)/shard_map/all_to_all | solution.py:63
  218.6 199.2 %reduce-scatter.2.cloned.1.call-start = ((), (), s32[]{:S(2)}) async-start(), calls=%async_computation.3 | async-start | bytes 573440 | tf_op jit(solution)/shard_map/reduce_scatter | solution.py:70
Sparse Core Ops, SparseCore 0:
  397.8 19.8 reduce-scatter.1
where the time goes:
time: 425 us
  waiting for transfers between devices  180 us (42%)
  blocking collectives  175 us (41%)
  local copies, waits for them, and re-layouts  23.9 us (6%)
  matrix products  16.5 us (4%)
  between operations  13.5 us (3%)
  other arithmetic  10.4 us (2%)
  starting transfers between devices  5.2 us (1%)
    all_to_all x1, blocking collectives, body(): lax.all_to_all(buffer, 'ep', split_axis=0, concat_axis=0, tiled=True)  167 us
    all_to_all x1, waiting for transfers between devices, body(): lax.all_to_all(result, 'ep', split_axis=0, concat_axis=0, tiled=True)  160 us
    reduce_scatter x1, waiting for transfers between devices, body(): lax.psum_scatter(combined.astype(jnp.bfloat16), 'dp', scatter_dimension=0...  20 us
    dot_general x1, matrix products, expert_apply(): jnp.einsum('sjnf,jfd->sjnd', hidden_part, down_mat, preferred_element_typ...  12.3 us
    gather x1, local copies, waits for them, and re-layouts, body(): picked = jnp.take(table, safe_targets, axis=0).astype(jnp.float32)  11.9 us
  transfers between devices with their start and end apart: 2, of which 2 were waited for; matrix products, arithmetic and copies ran while one was open for 0% of the time, Pallas kernels for 0%

commit v1 on v0

--- a/solution.py
+++ b/solution.py
@@ -40,7 +40,7 @@
     ).astype(jnp.bfloat16)
 
 
-def body(tokens, expert_ids, gate_weights, live_counts, w_gate, w_up, w_down):
+def slot_body(tokens, expert_ids, gate_weights, live_counts, w_gate, w_up, w_down):
     ep_count = lax.axis_size("ep")
     local_experts = w_gate.shape[0]
     experts_all = local_experts * ep_count
@@ -73,6 +73,48 @@
     return own_rows
 
 
+def dense_weights(block_ids, gate_weights, block_counts, experts_all):
+    rows = block_ids.shape[0]
+    per_device = rows // block_counts.shape[0]
+    position = jnp.arange(rows, dtype=jnp.int32)
+    limits = jnp.repeat(block_counts, per_device)
+    live = (position % per_device) < limits
+    named = block_ids[:, :, None] == jnp.arange(experts_all, dtype=jnp.int32)[None, None, :]
+    weights = jnp.where(named & live[:, None, None], gate_weights[:, :, None], 0.0)
+    return jnp.sum(weights, axis=1)
+
+
+def dense_body(tokens, expert_ids, gate_weights, live_counts, w_gate, w_up, w_down):
+    ep_count = lax.axis_size("ep")
+    local_experts = w_gate.shape[0]
+    experts_all = local_experts * ep_count
+    own = dense_weights(expert_ids, gate_weights, live_counts, experts_all)
+    first = lax.axis_index("ep") * local_experts
+    table = lax.all_gather(own, "ep", axis=0, tiled=True)
+    table = lax.dynamic_slice_in_dim(table, first, local_experts, axis=1)
+    everyone = lax.all_gather(tokens, ("ep", "dp"), axis=0, tiled=True)
+    total = None
+    for j in range(local_experts):
+        gate = jnp.dot(everyone, w_gate[j], preferred_element_type=jnp.float32)
+        up = jnp.dot(everyone, w_up[j], preferred_element_type=jnp.float32)
+        hidden = (jax.nn.silu(gate) * up * table[:, j : j + 1]).astype(jnp.bfloat16)
+        part = jnp.dot(hidden, w_down[j], preferred_element_type=jnp.float32)
+        total = part if total is None else total + part
+    partial = lax.psum_scatter(
+        total.astype(jnp.bfloat16), "ep", scatter_dimension=0, tiled=True
+    )
+    return lax.psum_scatter(partial, "dp", scatter_dimension=0, tiled=True)
+
+
+def body(tokens, expert_ids, gate_weights, live_counts, w_gate, w_up, w_down):
+    operands = (tokens, expert_ids, gate_weights, live_counts, w_gate, w_up, w_down)
+    experts_all = w_gate.shape[0] * lax.axis_size("ep")
+    capacity = 2 * expert_ids.shape[0] * expert_ids.shape[1] // experts_all
+    if capacity >= expert_ids.shape[0]:
+        return dense_body(*operands)
+    return slot_body(*operands)
+
+
 def solution(mesh):
     placed = (
         P(("ep", "dp"), None),

time: 425 us -> 210 us (0.49)
  blocking collectives: 175 us -> 32.3 us
  waiting for transfers between devices: 180 us -> 136 us
  local copies, waits for them, and re-layouts: 23.9 us -> 1.84 us
  other arithmetic: 10.4 us -> 0.74 us
  matrix products: 16.5 us -> 26.1 us
  starting transfers between devices: 5.2 us -> 0.08 us
    all_to_all x1 -> x0, blocking collectives: 167 us -> none  [body(): lax.all_to_all(buffer, 'ep', split_axis=0, concat_axis=0, tiled=True)]
    all_to_all x1 -> x0, waiting for transfers between devices: 160 us -> none  [body(): lax.all_to_all(result, 'ep', split_axis=0, concat_axis=0, tiled=True)]
    reduce_scatter x1 -> x2, waiting for transfers between devices: 20 us -> 103 us  [the longest x1 79.7 us: dense_body(): lax.psum_scatter(total.astype(jnp.bfloat16), 'ep', scatter_dimension=0, t...]
    all_gather x0 -> x1, waiting for transfers between devices: none -> 32 us  [dense_body(): everyone = lax.all_gather(tokens, ('ep', 'dp'), axis=0, tiled=True)]
    all_gather x1, blocking collectives: 8.47 us -> 32.3 us  [dense_body(): table = lax.all_gather(own, 'ep', axis=0, tiled=True)]
    gather x1 -> x0, local copies, waits for them, and re-layouts: 11.9 us -> none  [body(): picked = jnp.take(table, safe_targets, axis=0).astype(jnp.float32)]
    dot_general x3 -> x4, matrix products: 16.5 us -> 26.1 us  [the longest x2 21.1 us: dense_body(): part = jnp.dot(hidden, w_down[j], preferred_element_type=jnp.float32)]
    reduce_sum x4 -> x1, other arithmetic: 8.47 us -> 0.73 us  [dense_weights(): return jnp.sum(weights, axis=1)]
  transfers between devices with their start and end apart: 2 -> 3, of which waited for: 2 -> 3; matrix products, arithmetic and copies ran while one was open for 0% -> 1% of each run, Pallas kernels for 0% -> 0%
where the time goes in v1:
time: 210 us
  waiting for transfers between devices  136 us (65%)
  blocking collectives  32.3 us (15%)
  matrix products  26.1 us (12%)
  between operations  13.1 us (6%)
    reduce_scatter x1, waiting for transfers between devices, dense_body(): lax.psum_scatter(total.astype(jnp.bfloat16), 'ep', scatter_dimension=0, t...  79.7 us
    all_gather x1, blocking collectives, dense_body(): table = lax.all_gather(own, 'ep', axis=0, tiled=True)  32.3 us
    all_gather x1, waiting for transfers between devices, dense_body(): everyone = lax.all_gather(tokens, ('ep', 'dp'), axis=0, tiled=True)  32 us
    reduce_scatter x1, waiting for transfers between devices, dense_body(): return lax.psum_scatter(partial, 'dp', scatter_dimension=0, tiled=True)  23.5 us
    dot_general x2, matrix products, dense_body(): part = jnp.dot(hidden, w_down[j], preferred_element_type=jnp.float32)  21.1 us
    dot_general x2, matrix products, dense_body(): gate = jnp.dot(everyone, w_gate[j], preferred_element_type=jnp.float32)  4.97 us
  transfers between devices with their start and end apart: 3, of which 3 were waited for; matrix products, arithmetic and copies ran while one was open for 1% of the time, Pallas kernels for 0%

profile of v1, /device:TPU:0, one launch (start us, length us, event | category | flops | bytes accessed | tf_op | source)
XLA Modules:
  0.0 210.2 jit_solution(1002779079093533558)
XLA Ops:
  6.5 0.0 all-gather.3.cloned.1.call-start
  6.5 0.7 all-gather.3.cloned.1.call-update
  7.3 0.0 reduce-scatter.3.cloned.1.call-start
  7.3 0.7 broadcast_in_dim.19
  8.0 0.1 reshape.19
  8.1 0.7 select_reduce_fusion
  8.9 32.3 %all-gather = f32[8,64,16]{1,2,0:T(8,128)S(1)} all-gather(f32[1,64,16]{1,2,0:T(8,128)S(1)} %bitcast.43), channel_id=1, replica_groups=mesh['ep'=8,'dp'=4] {'ep'}, dimensions={0}, use_global_device_ids=true | all-gather | bytes 36864 | tf_op jit(solution)/shard_map/all_gather | solution.py:93
  41.2 0.1 reshape.21
  41.3 32.0 %all-gather.3.cloned.1.call-done = bf16[512,3584]{1,0:T(8,128)(2,1)} async-done(((bf16[16,3584]{1,0:T(8,128)(2,1)}), bf16[512,3584]{1,0:T(8,128)(2,1)}) %all-gather.3.cloned.1.call-update) | async-done | bytes 3670032 | tf_op jit(solution)/shard_map/all_gather | solution.py:95
  73.3 0.0 copy-start
  73.3 0.0 copy-start.1
  73.3 3.9 %fusion.3 = f32[512,256]{1,0:T(8,128)S(1)} fusion(bf16[512,3584]{1,0:T(8,128)(2,1)} %all-gather.3.cloned.1.call-done, bf16[2,3584,256]{2,1,0:T(8,128)(2,1)} %param.11), kind=kOutput, calls=%fused_computation.4 | convolution fusion | flops 939524096 | bytes 6029312 | tf_op jit(solution)/shard_map/dot_general | solution.py:98
  77.2 0.0 copy-done
  77.2 0.9 copy-done.1
  78.1 1.1 fusion.9
  79.3 10.0 %fusion.5 = f32[512,3584]{1,0:T(8,128)} fusion(bf16[2,256,3584]{2,1,0:T(8,128)(2,1)} %param.13, bf16[512,3584]{1,0:T(8,128)(2,1)} %all-gather.3.cloned.1.call-done, bf16[2,3584,256]{2,1,0:T(8,128)(2,1)} %param.12, f32[512,256]{1,0:T(8,128)S(1)} %fusion.9, f32[512]{0:T(512)S(1)} %bitcast.45), kind=kOutput, calls=%fused_computation.6 | convolution fusion | flops 1879965696 | bytes 15206400 | tf_op jit(solution)/shard_map/dot_general | solution.py:101
  89.3 11.1 %add_convert_fusion = bf16[512,3584]{1,0:T(8,128)(2,1)} fusion(f32[512,3584]{1,0:T(8,128)} %fusion.5, bf16[2,256,3584]{2,1,0:T(8,128)(2,1)} %param.13, bf16[512,3584]{1,0:T(8,128)(2,1)} %all-gather.3.cloned.1.call-done, bf16[2,3584,256]{2,1,0:T(8,128)(2,1)} %param.12, f32[512,256]{1,0:T(8,128)S(1)} %fusion.3, f32[512]{0:T(512)S(1)} %bitcast.44), kind=kOutput, calls=%fused_computation | convolution fusion | flops 1883635712 | bytes 18876416 | tf_op jit(solution)/shard_map/dot_general | solution.py:101
  100.4 0.0 reduce-scatter.3.cloned.1.call-update
  100.4 0.0 reduce-scatter.5.cloned.1.call-start
  100.4 79.7 %reduce-scatter.3.cloned.1.call-done = bf16[64,3584]{1,0:T(8,128)(2,1)} async-done(((bf16[512,3584]{1,0:T(8,128)(2,1)}), bf16[64,3584]{1,0:T(8,128)(2,1)}) %reduce-scatter.3.cloned.1.call-update) | async-done | bytes 458768 | tf_op jit(solution)/shard_map/reduce_scatter | solution.py:103
  180.2 0.0 reduce-scatter.5.cloned.1.call-update
  180.2 23.5 %reduce-scatter.5.cloned.1.call-done = bf16[16,3584]{1,0:T(8,128)(2,1)} async-done(((bf16[64,3584]{1,0:T(8,128)(2,1)}), bf16[16,3584]{1,0:T(8,128)(2,1)}) %reduce-scatter.5.cloned.1.call-update) | async-done | bytes 114704 | tf_op jit(solution)/shard_map/reduce_scatter | solution.py:106
  (3 shorter events, 0.0 us)
Async XLA Ops:
  6.5 66.8 %all-gather.3.cloned.1.call-start = ((), (), s32[]{:S(2)}) async-start(), calls=%async_computation.2 | async-start | bytes 3784704 | tf_op jit(solution)/shard_map/all_gather | solution.py:95
  7.3 172.9 %reduce-scatter.3.cloned.1.call-start = ((), (), s32[]{:S(2)}) async-start(), calls=%async_computation.3 | async-start | bytes 4128768 | tf_op jit(solution)/shard_map/reduce_scatter | solution.py:103
  73.3 3.9 %copy-start = (bf16[512,3584]{1,0:T(8,128)(2,1)S(1)}, bf16[512,3584]{1,0:T(8,128)(2,1)}, u32[]{:S(2)}) copy-start(bf16[512,3584]{1,0:T(8,128)(2,1)} %all-gather.3.cloned.1.call-done) | copy-start | bytes 11010052
  73.3 4.8 %copy-start.1 = (bf16[2,3584,256]{2,1,0:T(8,128)(2,1)S(1)}, bf16[2,3584,256]{2,1,0:T(8,128)(2,1)}, u32[]{:S(2)}) copy-start(bf16[2,3584,256]{2,1,0:T(8,128)(2,1)} %param.11) | copy-start | bytes 11010052
  100.4 103.3 %reduce-scatter.5.cloned.1.call-start = ((), (), s32[]{:S(2)}) async-start(), calls=%async_computation.4 | async-start | bytes 573440 | tf_op jit(solution)/shard_map/reduce_scatter | solution.py:106
Sparse Core Ops, SparseCore 0:
  10.2 63.0 all-gather.2
  100.5 79.6 reduce-scatter.2
  182.7 20.9 reduce-scatter.4

commit v2 on v0

--- a/solution.py
+++ b/solution.py
@@ -1,6 +1,8 @@
 import jax
 import jax.numpy as jnp
 from jax import lax
+from jax.experimental import pallas as pl
+from jax.experimental.pallas import tpu as pltpu
 from jax.sharding import PartitionSpec as P
 
 
@@ -40,7 +42,7 @@
     ).astype(jnp.bfloat16)
 
 
-def body(tokens, expert_ids, gate_weights, live_counts, w_gate, w_up, w_down):
+def slot_body(tokens, expert_ids, gate_weights, live_counts, w_gate, w_up, w_down):
     ep_count = lax.axis_size("ep")
     local_experts = w_gate.shape[0]
     experts_all = local_experts * ep_count
@@ -73,6 +75,273 @@
     return own_rows
 
 
+MESH = pl.DeviceIdType.MESH
+LANES = 128
+CHUNKS = 4
+
+
+def fused_kernel(
+    tokens_ref, ids_ref, gates_ref, counts_ref, gate_hbm, up_hbm, down_hbm, out_ref,
+    table, partial, from_core, from_diag, from_side, from_line,
+    gate_mat, up_mat, down_mat, load_sem, gs, gr, rs, rr,
+):
+    depth = lax.axis_size("ep") // 2
+    rows, width = tokens_ref.shape
+    local_experts, _, hidden = gate_hbm.shape
+    experts_all = local_experts * lax.axis_size("ep")
+    ep, dp = lax.axis_index("ep"), lax.axis_index("dp")
+    z, y, x, c = ep // 2, ep % 2, dp // 2, dp % 2
+    full = width + LANES
+    half = (width // LANES // 2) * LANES
+
+    loads = []
+    for j in range(local_experts):
+        down_rows = down_mat.at[pl.ds(j * hidden, hidden)]
+        loads += [(gate_hbm.at[j], gate_mat.at[j]), (up_hbm.at[j], up_mat.at[j]), (down_hbm.at[j], down_rows)]
+    loads = [pltpu.make_async_copy(s, d, load_sem.at[i]) for i, (s, d) in enumerate(loads)]
+    for load in loads:
+        load.start()
+
+    def place(core, py, px, pz):
+        return pl.multiple_of((((core * 2 + py) * 2 + px) * depth + pz) * rows, rows)
+
+    def device(pz, py, px, core):
+        return (pz * 2 + py, px * 2 + core)
+
+    y_peer, x_peer = device(z, 1 - y, x, c), device(z, y, 1 - x, c)
+    core_peer = device(z, y, x, 1 - c)
+    hops = [(z + k) % depth for k in range(depth)]
+    came = [(z + depth - k) % depth for k in range(depth)]
+    line = [device(hops[k], y, x, c) for k in range(1, depth)]
+
+    mine = pl.ds(place(c, y, x, z), rows)
+    table[mine, 0:width] = tokens_ref[...]
+    own = pl.ds(pl.multiple_of(dp * rows, rows), rows)
+    ids, gates = ids_ref[own, :], gates_ref[own, :]
+    lane = lax.broadcasted_iota(jnp.int32, (rows, LANES), 1)
+    live = lax.broadcasted_iota(jnp.int32, (rows, LANES), 0) < counts_ref[dp]
+    expert = jnp.where(lane < experts_all, lane, lane - experts_all)
+    weight = jnp.zeros((rows, LANES), jnp.float32)
+    for k in range(ids.shape[1]):
+        weight += jnp.where(ids[:, k : k + 1] == expert, gates[:, k : k + 1], 0.0)
+    weight = jnp.where(live, weight, 0.0)
+    high = weight.astype(jnp.bfloat16).astype(jnp.float32)
+    split = jnp.where(lane < experts_all, high, weight - high)
+    table[mine, width:full] = jnp.where(lane < 2 * experts_all, split, 0.0).astype(jnp.bfloat16)
+
+    barrier = pltpu.get_barrier_semaphore()
+    peers = line + [y_peer, x_peer, core_peer]
+    for peer in peers:
+        pl.semaphore_signal(barrier, inc=1, device_id=peer, device_id_type=MESH)
+    pl.semaphore_wait(barrier, len(peers))
+
+    def remote(source, target, send, recv, peer):
+        return pltpu.make_async_remote_copy(
+            src_ref=source, dst_ref=target, send_sem=send, recv_sem=recv,
+            device_id=peer, device_id_type=MESH,
+        )
+
+    def spread(kind, k, start, lo, hi, peer):
+        piece = table.at[pl.ds(start, rows), lo:hi]
+        return remote(piece, piece, gs.at[kind, k], gr.at[kind, k], peer)
+
+    sent = []
+
+    def send(*what):
+        copy = spread(*what)
+        copy.start()
+        sent.append(copy)
+
+    start_own = place(c, y, x, z)
+    for k in range(1, depth):
+        send(0, k, start_own, 0, full, line[k - 1])
+    for k in range(depth):
+        here = place(c, y, x, came[k])
+        if k > 0:
+            spread(0, k, here, 0, full, core_peer).wait_recv()
+        send(1, k, here, 0, full, y_peer)
+        send(2, k, here, 0, full, x_peer)
+        send(5, k, here, 0, full, core_peer)
+    for k in range(depth):
+        here = place(c, 1 - y, x, came[k])
+        spread(1, k, here, 0, full, y_peer).wait_recv()
+        send(3, k, here, 0, half, x_peer)
+        send(6, k, here, 0, full, core_peer)
+        here = place(c, y, 1 - x, came[k])
+        spread(2, k, here, 0, full, x_peer).wait_recv()
+        send(4, k, here, half, full, y_peer)
+        send(7, k, here, 0, full, core_peer)
+    for k in range(depth):
+        here = place(c, 1 - y, 1 - x, came[k])
+        spread(3, k, here, 0, half, x_peer).wait_recv()
+        spread(4, k, here, half, full, y_peer).wait_recv()
+        send(8, k, here, 0, full, core_peer)
+    for load in loads:
+        load.wait()
+    sides = [(y, x), (1 - y, x), (y, 1 - x), (1 - y, 1 - x)]
+    for kind, (py, px) in enumerate(sides):
+        for k in range(depth):
+            spread(5 + kind, k, place(1 - c, py, px, came[k]), 0, full, core_peer).wait_recv()
+
+    block = depth * rows
+    chunk = 2 * block
+    first = ep * local_experts
+    tile = 512 if width % 512 == 0 else LANES
+
+    def across(i, py):
+        piece = pl.ds(place(1 - c, py, 0, 0), chunk)
+        landing = pl.ds(pl.multiple_of(py * chunk, chunk), chunk)
+        return remote(partial.at[piece], from_core.at[landing], rs.at[0, i], rr.at[0, i], core_peer)
+
+    def corner(side):
+        lo, hi = (0, half) if side == 0 else (half, width)
+        piece = partial.at[pl.ds(place(c, 1 - y, 1 - x, 0), block), lo:hi]
+        peer = x_peer if side == 0 else y_peer
+        return remote(piece, from_diag.at[:, lo:hi], rs.at[1, side], rr.at[1, side], peer)
+
+    def compute(i, _):
+        core = jnp.where(i < 2, 1 - c, c)
+        py = jnp.where(i % 2 == 0, 1 - y, y)
+        start = place(core, py, 0, 0)
+        span = pl.ds(start, chunk)
+        extra = table[span, width:full].astype(jnp.float32)
+        lanes = lax.broadcasted_iota(jnp.int32, (chunk, LANES), 1)
+        parts = []
+        for j in range(local_experts):
+            pick = (lanes == first + j) | (lanes == experts_all + first + j)
+            share = jnp.sum(jnp.where(pick, extra, 0.0), axis=1, keepdims=True)
+            gate = jnp.dot(table[span, 0:width], gate_mat[j], preferred_element_type=jnp.float32)
+            up = jnp.dot(table[span, 0:width], up_mat[j], preferred_element_type=jnp.float32)
+            parts.append((gate / (1.0 + jnp.exp(-gate)) * up * share).astype(jnp.bfloat16))
+        both = jnp.concatenate(parts, axis=1)
+
+        @pl.loop(0, width // tile)
+        def _(n):
+            columns = pl.ds(pl.multiple_of(n * tile, tile), tile)
+            partial[span, columns] = jnp.dot(
+                both, down_mat[:, columns], preferred_element_type=jnp.float32
+            ).astype(jnp.bfloat16)
+
+        @pl.when(i < 2)
+        def _():
+            across(i, py).start()
+
+        @pl.when(i >= 2)
+        def _():
+            across(i - 2, py).wait_recv()
+
+            @pl.loop(0, chunk // rows)
+            def _(r):
+                here = pl.ds(pl.multiple_of(start + r * rows, rows), rows)
+                there = pl.ds(pl.multiple_of(py * chunk + r * rows, rows), rows)
+                total = partial[here, :].astype(jnp.float32) + from_core[there, :].astype(jnp.float32)
+                partial[here, :] = total.astype(jnp.bfloat16)
+
+        @pl.when(i == 2)
+        def _():
+            corner(0).start()
+            corner(1).start()
+
+        return 0
+
+    lax.fori_loop(0, CHUNKS, compute, 0)
+
+    def side_copy(side):
+        start = place(c, 1 - y, x, 0) if side == 0 else place(c, y, 1 - x, 0)
+        piece = partial.at[pl.ds(start, block)]
+        peer = y_peer if side == 0 else x_peer
+        return remote(piece, from_side.at[side], rs.at[2, side], rr.at[2, side], peer)
+
+    for side in range(2):
+        corner(side).wait_recv()
+        lo, hi = (0, half) if side == 0 else (half, width)
+        start = place(c, 1 - y, x, 0) if side == 0 else place(c, y, 1 - x, 0)
+        for k in range(depth):
+            here = pl.ds(pl.multiple_of(start + k * rows, rows), rows)
+            there = pl.ds(k * rows, rows)
+            total = partial[here, lo:hi].astype(jnp.float32) + from_diag[there, lo:hi].astype(jnp.float32)
+            partial[here, lo:hi] = total.astype(jnp.bfloat16)
+        side_copy(side).start()
+    side_copy(0).wait_recv()
+    side_copy(1).wait_recv()
+
+    def line_copy(k):
+        piece = partial.at[pl.ds(place(c, y, x, hops[k]), rows)]
+        return remote(piece, from_line.at[k - 1], rs.at[3, k], rr.at[3, k], line[k - 1])
+
+    def settle(pz):
+        here = pl.ds(place(c, y, x, pz), rows)
+        there = pl.ds(pl.multiple_of(pz * rows, rows), rows)
+        total = partial[here, :].astype(jnp.float32) + from_side[0, there, :].astype(jnp.float32)
+        return total + from_side[1, there, :].astype(jnp.float32)
+
+    for k in range(1, depth):
+        partial[pl.ds(place(c, y, x, hops[k]), rows), :] = settle(hops[k]).astype(jnp.bfloat16)
+        line_copy(k).start()
+    total = settle(z)
+    for k in range(1, depth):
+        line_copy(k).wait_recv()
+        total += from_line[k - 1].astype(jnp.float32)
+    out_ref[...] = total.astype(out_ref.dtype)
+
+    for copy in sent:
+        copy.wait_send()
+    across(0, 1 - y).wait_send()
+    across(1, y).wait_send()
+    for side in range(2):
+        corner(side).wait_send()
+        side_copy(side).wait_send()
+    for k in range(1, depth):
+        line_copy(k).wait_send()
+
+
+def fused_body(tokens, expert_ids, gate_weights, live_counts, w_gate, w_up, w_down):
+    depth = lax.axis_size("ep") // 2
+    rows, width = tokens.shape
+    local_experts, _, hidden = w_gate.shape
+    everyone = depth * 8 * rows
+    vmem, hbm = pl.BlockSpec(memory_space=pltpu.VMEM), pl.BlockSpec(memory_space=pl.ANY)
+    weights = local_experts * width * hidden
+    return pl.pallas_call(
+        fused_kernel,
+        out_shape=jax.ShapeDtypeStruct((rows, width), tokens.dtype),
+        in_specs=[vmem, vmem, vmem, pl.BlockSpec(memory_space=pltpu.SMEM), hbm, hbm, hbm],
+        out_specs=vmem,
+        scratch_shapes=[
+            pltpu.VMEM((everyone, width + LANES), jnp.bfloat16),
+            pltpu.VMEM((everyone, width), jnp.bfloat16),
+            pltpu.VMEM((everyone // 2, width), jnp.bfloat16),
+            pltpu.VMEM((depth * rows, width), jnp.bfloat16),
+            pltpu.VMEM((2, depth * rows, width), jnp.bfloat16),
+            pltpu.VMEM((depth - 1, rows, width), jnp.bfloat16),
+            pltpu.VMEM((local_experts, width, hidden), jnp.bfloat16),
+            pltpu.VMEM((local_experts, width, hidden), jnp.bfloat16),
+            pltpu.VMEM((local_experts * hidden, width), jnp.bfloat16),
+            pltpu.SemaphoreType.DMA((3 * local_experts,)),
+            pltpu.SemaphoreType.DMA((9, depth)),
+            pltpu.SemaphoreType.DMA((9, depth)),
+            pltpu.SemaphoreType.DMA((4, max(depth, 2))),
+            pltpu.SemaphoreType.DMA((4, max(depth, 2))),
+        ],
+        compiler_params=pltpu.CompilerParams(
+            collective_id=0, has_side_effects=True, vmem_limit_bytes=56 << 20
+        ),
+        cost_estimate=pl.CostEstimate(
+            flops=6 * everyone * weights, bytes_accessed=6 * weights, transcendentals=0
+        ),
+    )(tokens, expert_ids, gate_weights, live_counts, w_gate, w_up, w_down)
+
+
+def body(tokens, expert_ids, gate_weights, live_counts, w_gate, w_up, w_down):
+    operands = (tokens, expert_ids, gate_weights, live_counts, w_gate, w_up, w_down)
+    ep_count, dp_count = lax.axis_size("ep"), lax.axis_size("dp")
+    experts_all = w_gate.shape[0] * ep_count
+    capacity = 2 * expert_ids.shape[0] * expert_ids.shape[1] // experts_all
+    if capacity >= expert_ids.shape[0] and ep_count == 8 and dp_count == 4:
+        return fused_body(*operands)
+    return slot_body(*operands)
+
+
 def solution(mesh):
     placed = (
         P(("ep", "dp"), None),

time: 425 us -> 72 us (0.17)
  waiting for transfers between devices: 180 us -> 0 us
  blocking collectives: 175 us -> 0 us
  Pallas kernels: 0 us -> 67.5 us
  local copies, waits for them, and re-layouts: 23.9 us -> 4.31 us
  matrix products: 16.5 us -> 0 us
  between operations: 13.5 us -> 0.01 us
  other arithmetic: 10.4 us -> 0 us
  starting transfers between devices: 5.2 us -> 0 us
    all_to_all x1 -> x0, blocking collectives: 167 us -> none  [body(): lax.all_to_all(buffer, 'ep', split_axis=0, concat_axis=0, tiled=True)]
    all_to_all x1 -> x0, waiting for transfers between devices: 160 us -> none  [body(): lax.all_to_all(result, 'ep', split_axis=0, concat_axis=0, tiled=True)]
    pallas_call x0 -> x1, Pallas kernels: none -> 67.5 us  [fused_body(): pl.pallas_call(fused_kernel, out_shape=jax.ShapeDtypeStruct((rows, width)...]
    reduce_scatter x1 -> x0, waiting for transfers between devices: 20 us -> none  [body(): lax.psum_scatter(combined.astype(jnp.bfloat16), 'dp', scatter_dimension=0...]
    dot_general x3 -> x0, matrix products: 16.5 us -> none  [the longest x1 12.3 us: expert_apply(): jnp.einsum('sjnf,jfd->sjnd', hidden_part, down_mat, preferred_element_typ...]
    gather x1 -> x0, local copies, waits for them, and re-layouts: 11.9 us -> none  [body(): picked = jnp.take(table, safe_targets, axis=0).astype(jnp.float32)]
    all_gather x1 -> x0, blocking collectives: 8.47 us -> none  [body(): block_tokens = lax.all_gather(tokens, 'dp', axis=0, tiled=True)]
    reduce_sum x4 -> x0, other arithmetic: 8.47 us -> none  [the longest x1 6.95 us: body(): combined = jnp.sum(weights[:, :, None] * picked, axis=1)]
  transfers between devices with their start and end apart: 2 -> 0, of which waited for: 2 -> 0; matrix products, arithmetic and copies ran while one was open for 0% -> 0% of each run, Pallas kernels for 0% -> 0%
where the time goes in v2:
time: 72 us; the launch traced here: 71.8 us
  Pallas kernels  67.5 us (94%)
  local copies, waits for them, and re-layouts  4.31 us (6%)
    pallas_call x1, Pallas kernels, fused_body(): pl.pallas_call(fused_kernel, out_shape=jax.ShapeDtypeStruct((rows, width)...  67.5 us
    unnamed x3, local copies, waits for them, and re-layouts  4.31 us

profile of v2, /device:TPU:0, one launch (start us, length us, event | category | flops | bytes accessed | tf_op | source)
XLA Modules:
  0.0 71.8 jit_solution(17466948172363844929)
XLA Ops:
  0.0 1.4 %copy.8.ids_ref = s32[64,8]{1,0:T(8,128)} copy(s32[64,8]{0,1:T(8,128)} %param.8) | data formatting | bytes 4096 | tf_op args[1]
  1.4 1.4 %copy.9.gates_ref = f32[64,8]{1,0:T(8,128)} copy(f32[64,8]{0,1:T(8,128)} %param.9) | data formatting | bytes 4096 | tf_op args[2]
  2.8 67.5 %shard_map.73 = bf16[16,3584]{1,0:T(8,128)(2,1)} custom-call(bf16[16,3584]{1,0:T(8,128)(2,1)} %tokens_ref.1, s32[64,8]{1,0:T(8,128)} %copy.8.ids_ref, f32[64,8]{1,0:T(8,128)} %copy.9.gates_ref, s32[4]{0:T(128)} %counts_ref.1, bf16[2,3584,256]{2,1,0:T(8,128)(2,1)} %gate_hbm.1, bf16[2,3584,256]{2,1,0:T(8,128)(2,1)} %up_hbm.1, bf16[2,256,3584]{2,1,0:T(8,128)(2,1)} %down_hbm.1), custom_call_target="tpu_custom_call" | custom-call | flops 5637144576 | bytes 11010048 | tf_op jit(solution)/shard_map/pallas_call | solution.py:305
  70.2 1.6 %copy.11 = bf16[16,3584]{1,0:T(8,128)(2,1)} copy(bf16[16,3584]{1,0:T(8,128)(2,1)} %shard_map.73) | data formatting | bytes 229376

commit v3 on v2

--- a/solution.py
+++ b/solution.py
@@ -77,13 +77,12 @@
 
 MESH = pl.DeviceIdType.MESH
 LANES = 128
-CHUNKS = 4
 
 
 def fused_kernel(
     tokens_ref, ids_ref, gates_ref, counts_ref, gate_hbm, up_hbm, down_hbm, out_ref,
     table, partial, from_core, from_diag, from_side, from_line,
-    gate_mat, up_mat, down_mat, load_sem, gs, gr, rs, rr,
+    gate_mat, up_mat, down_mat, hidden_rows, load_sem, gs, gr, rs, rr,
 ):
     depth = lax.axis_size("ep") // 2
     rows, width = tokens_ref.shape
@@ -103,7 +102,7 @@
         load.start()
 
     def place(core, py, px, pz):
-        return pl.multiple_of((((core * 2 + py) * 2 + px) * depth + pz) * rows, rows)
+        return pl.multiple_of((((py * 2 + core) * 2 + px) * depth + pz) * rows, rows)
 
     def device(pz, py, px, core):
         return (pz * 2 + py, px * 2 + core)
@@ -116,18 +115,23 @@
 
     mine = pl.ds(place(c, y, x, z), rows)
     table[mine, 0:width] = tokens_ref[...]
-    own = pl.ds(pl.multiple_of(dp * rows, rows), rows)
-    ids, gates = ids_ref[own, :], gates_ref[own, :]
-    lane = lax.broadcasted_iota(jnp.int32, (rows, LANES), 1)
-    live = lax.broadcasted_iota(jnp.int32, (rows, LANES), 0) < counts_ref[dp]
-    expert = jnp.where(lane < experts_all, lane, lane - experts_all)
-    weight = jnp.zeros((rows, LANES), jnp.float32)
-    for k in range(ids.shape[1]):
-        weight += jnp.where(ids[:, k : k + 1] == expert, gates[:, k : k + 1], 0.0)
-    weight = jnp.where(live, weight, 0.0)
+    ids, gates = ids_ref[...], gates_ref[...]
+    top, group = ids.shape
+    code = lax.broadcasted_iota(jnp.int32, (LANES, group), 0)
+    expert = jnp.where(code < experts_all, code, code - experts_all)
+    weight = jnp.zeros((LANES, group), jnp.float32)
+    for k in range(top):
+        weight += jnp.where(ids[k : k + 1, :] == expert, gates[k : k + 1, :], 0.0)
     high = weight.astype(jnp.bfloat16).astype(jnp.float32)
-    split = jnp.where(lane < experts_all, high, weight - high)
-    table[mine, width:full] = jnp.where(lane < 2 * experts_all, split, 0.0).astype(jnp.bfloat16)
+    split = jnp.where(code < experts_all, high, weight - high)
+    split = jnp.where(code < 2 * experts_all, split, 0.0).astype(jnp.bfloat16)
+    row = lax.broadcasted_iota(jnp.int32, (rows, group), 0)
+    column = lax.broadcasted_iota(jnp.int32, (rows, group), 1)
+    live = (column == dp * rows + row) & (row < counts_ref[dp])
+    table[mine, width:full] = lax.dot_general(
+        jnp.where(live, 1.0, 0.0).astype(jnp.bfloat16), split,
+        (((1,), (1,)), ((), ())), preferred_element_type=jnp.float32,
+    ).astype(jnp.bfloat16)
 
     barrier = pltpu.get_barrier_semaphore()
     peers = line + [y_peer, x_peer, core_peer]
@@ -171,114 +175,141 @@
         spread(2, k, here, 0, full, x_peer).wait_recv()
         send(4, k, here, half, full, y_peer)
         send(7, k, here, 0, full, core_peer)
-    for k in range(depth):
-        here = place(c, 1 - y, 1 - x, came[k])
-        spread(3, k, here, 0, half, x_peer).wait_recv()
-        spread(4, k, here, half, full, y_peer).wait_recv()
-        send(8, k, here, 0, full, core_peer)
-    for load in loads:
-        load.wait()
-    sides = [(y, x), (1 - y, x), (y, 1 - x), (1 - y, 1 - x)]
-    for kind, (py, px) in enumerate(sides):
+
+    def finish_gather():
         for k in range(depth):
-            spread(5 + kind, k, place(1 - c, py, px, came[k]), 0, full, core_peer).wait_recv()
+            here = place(c, 1 - y, 1 - x, came[k])
+            spread(3, k, here, 0, half, x_peer).wait_recv()
+            spread(4, k, here, half, full, y_peer).wait_recv()
+            send(8, k, here, 0, full, core_peer)
+
+    def meet(kind, py, px):
+        for k in range(depth):
+            spread(kind, k, place(1 - c, py, px, came[k]), 0, full, core_peer).wait_recv()
 
     block = depth * rows
     chunk = 2 * block
     first = ep * local_experts
     tile = 512 if width % 512 == 0 else LANES
+    order = list(range(1, depth)) + [0]
+
+    def emit(copy):
+        copy.start()
+        sent.append(copy)
 
     def across(i, py):
         piece = pl.ds(place(1 - c, py, 0, 0), chunk)
         landing = pl.ds(pl.multiple_of(py * chunk, chunk), chunk)
         return remote(partial.at[piece], from_core.at[landing], rs.at[0, i], rr.at[0, i], core_peer)
 
-    def corner(side):
+    def slot(py, px, k):
+        return pl.ds(place(c, py, px, hops[k]), rows)
+
+    def spot(k):
+        return pl.ds(pl.multiple_of(hops[k] * rows, rows), rows)
+
+    def corner(side, k):
         lo, hi = (0, half) if side == 0 else (half, width)
-        piece = partial.at[pl.ds(place(c, 1 - y, 1 - x, 0), block), lo:hi]
+        piece = partial.at[slot(1 - y, 1 - x, k), lo:hi]
+        landing = from_diag.at[spot(k), lo:hi]
         peer = x_peer if side == 0 else y_peer
-        return remote(piece, from_diag.at[:, lo:hi], rs.at[1, side], rr.at[1, side], peer)
-
-    def compute(i, _):
-        core = jnp.where(i < 2, 1 - c, c)
-        py = jnp.where(i % 2 == 0, 1 - y, y)
-        start = place(core, py, 0, 0)
-        span = pl.ds(start, chunk)
+        return remote(piece, landing, rs.at[1 + side, k], rr.at[1 + side, k], peer)
+
+    def side_copy(kind, k):
+        py, px, peer, side = (y, 1 - x, x_peer, 1) if kind < 5 else (1 - y, x, y_peer, 0)
+        lo, hi = (0, half) if kind in (3, 6) else (half, width)
+        piece = partial.at[slot(py, px, k), lo:hi]
+        landing = from_side.at[side, spot(k), lo:hi]
+        return remote(piece, landing, rs.at[kind, k], rr.at[kind, k], peer)
+
+    def add_core(py, px, k):
+        here = slot(py, px, k)
+        there = pl.ds(pl.multiple_of(((py * 2 + px) * depth + hops[k]) * rows, rows), rows)
+        total = partial[here, :].astype(jnp.float32) + from_core[there, :].astype(jnp.float32)
+        partial[here, :] = total.astype(jnp.bfloat16)
+
+    def early():
+        across(0, y).wait_recv()
+        for k in order:
+            add_core(y, 1 - x, k)
+            emit(side_copy(3, k))
+        for k in order:
+            add_core(y, x, k)
+
+    def compute(i, py, between, before_down):
+        start = place(0, py, 0, 0)
+        span = pl.ds(start, 2 * chunk)
         extra = table[span, width:full].astype(jnp.float32)
-        lanes = lax.broadcasted_iota(jnp.int32, (chunk, LANES), 1)
-        parts = []
+        lanes = lax.broadcasted_iota(jnp.int32, (2 * chunk, LANES), 1)
         for j in range(local_experts):
             pick = (lanes == first + j) | (lanes == experts_all + first + j)
             share = jnp.sum(jnp.where(pick, extra, 0.0), axis=1, keepdims=True)
             gate = jnp.dot(table[span, 0:width], gate_mat[j], preferred_element_type=jnp.float32)
             up = jnp.dot(table[span, 0:width], up_mat[j], preferred_element_type=jnp.float32)
-            parts.append((gate / (1.0 + jnp.exp(-gate)) * up * share).astype(jnp.bfloat16))
-        both = jnp.concatenate(parts, axis=1)
-
-        @pl.loop(0, width // tile)
-        def _(n):
-            columns = pl.ds(pl.multiple_of(n * tile, tile), tile)
-            partial[span, columns] = jnp.dot(
-                both, down_mat[:, columns], preferred_element_type=jnp.float32
-            ).astype(jnp.bfloat16)
-
-        @pl.when(i < 2)
-        def _():
-            across(i, py).start()
-
-        @pl.when(i >= 2)
-        def _():
-            across(i - 2, py).wait_recv()
-
-            @pl.loop(0, chunk // rows)
-            def _(r):
-                here = pl.ds(pl.multiple_of(start + r * rows, rows), rows)
-                there = pl.ds(pl.multiple_of(py * chunk + r * rows, rows), rows)
-                total = partial[here, :].astype(jnp.float32) + from_core[there, :].astype(jnp.float32)
-                partial[here, :] = total.astype(jnp.bfloat16)
-
-        @pl.when(i == 2)
-        def _():
-            corner(0).start()
-            corner(1).start()
-
-        return 0
-
-    lax.fori_loop(0, CHUNKS, compute, 0)
-
-    def side_copy(side):
-        start = place(c, 1 - y, x, 0) if side == 0 else place(c, y, 1 - x, 0)
-        piece = partial.at[pl.ds(start, block)]
-        peer = y_peer if side == 0 else x_peer
-        return remote(piece, from_side.at[side], rs.at[2, side], rr.at[2, side], peer)
-
-    for side in range(2):
-        corner(side).wait_recv()
-        lo, hi = (0, half) if side == 0 else (half, width)
-        start = place(c, 1 - y, x, 0) if side == 0 else place(c, y, 1 - x, 0)
-        for k in range(depth):
-            here = pl.ds(pl.multiple_of(start + k * rows, rows), rows)
-            there = pl.ds(k * rows, rows)
+            value = gate / (1.0 + jnp.exp(-gate)) * up * share
+            hidden_rows[:, j * hidden : (j + 1) * hidden] = value.astype(jnp.bfloat16)
+            if j == 0:
+                between()
+        before_down()
+        for core in (1 - c, c):
+            both = hidden_rows[pl.ds(pl.multiple_of(core * chunk, chunk), chunk), :]
+            target = pl.ds(place(core, py, 0, 0), chunk)
+
+            @pl.loop(0, width // tile)
+            def _(n):
+                columns = pl.ds(pl.multiple_of(n * tile, tile), tile)
+                partial[target, columns] = jnp.dot(
+                    both, down_mat[:, columns], preferred_element_type=jnp.float32
+                ).astype(jnp.bfloat16)
+
+            if core is not c:
+                emit(across(i, py))
+
+    def nothing():
+        pass
+
+    for load in loads:
+        load.wait()
+    meet(5, y, x)
+    meet(7, y, 1 - x)
+    compute(0, y, nothing, finish_gather)
+    meet(6, 1 - y, x)
+    meet(8, 1 - y, 1 - x)
+    compute(1, 1 - y, early, nothing)
+
+    across(1, 1 - y).wait_recv()
+    for k in order:
+        add_core(1 - y, 1 - x, k)
+        emit(corner(0, k))
+        emit(corner(1, k))
+    for k in order:
+        add_core(1 - y, x, k)
+        emit(side_copy(5, k))
+
+    for k in order:
+        for side, kind, py, px in ((0, 6, 1 - y, x), (1, 4, y, 1 - x)):
+            corner(side, k).wait_recv()
+            lo, hi = (0, half) if side == 0 else (half, width)
+            here, there = slot(py, px, k), spot(k)
             total = partial[here, lo:hi].astype(jnp.float32) + from_diag[there, lo:hi].astype(jnp.float32)
             partial[here, lo:hi] = total.astype(jnp.bfloat16)
-        side_copy(side).start()
-    side_copy(0).wait_recv()
-    side_copy(1).wait_recv()
+            emit(side_copy(kind, k))
 
     def line_copy(k):
-        piece = partial.at[pl.ds(place(c, y, x, hops[k]), rows)]
-        return remote(piece, from_line.at[k - 1], rs.at[3, k], rr.at[3, k], line[k - 1])
-
-    def settle(pz):
-        here = pl.ds(place(c, y, x, pz), rows)
-        there = pl.ds(pl.multiple_of(pz * rows, rows), rows)
-        total = partial[here, :].astype(jnp.float32) + from_side[0, there, :].astype(jnp.float32)
+        piece = partial.at[slot(y, x, k)]
+        return remote(piece, from_line.at[k - 1], rs.at[7, k], rr.at[7, k], line[k - 1])
+
+    def settle(k):
+        for kind in (3, 4, 5, 6):
+            side_copy(kind, k).wait_recv()
+        there = spot(k)
+        total = partial[slot(y, x, k), :].astype(jnp.float32) + from_side[0, there, :].astype(jnp.float32)
         return total + from_side[1, there, :].astype(jnp.float32)
 
     for k in range(1, depth):
-        partial[pl.ds(place(c, y, x, hops[k]), rows), :] = settle(hops[k]).astype(jnp.bfloat16)
-        line_copy(k).start()
-    total = settle(z)
+        partial[slot(y, x, k), :] = settle(k).astype(jnp.bfloat16)
+        emit(line_copy(k))
+    total = settle(0)
     for k in range(1, depth):
         line_copy(k).wait_recv()
         total += from_line[k - 1].astype(jnp.float32)
@@ -286,13 +317,6 @@
 
     for copy in sent:
         copy.wait_send()
-    across(0, 1 - y).wait_send()
-    across(1, y).wait_send()
-    for side in range(2):
-        corner(side).wait_send()
-        side_copy(side).wait_send()
-    for k in range(1, depth):
-        line_copy(k).wait_send()
 
 
 def fused_body(tokens, expert_ids, gate_weights, live_counts, w_gate, w_up, w_down):
@@ -317,11 +341,12 @@
             pltpu.VMEM((local_experts, width, hidden), jnp.bfloat16),
             pltpu.VMEM((local_experts, width, hidden), jnp.bfloat16),
             pltpu.VMEM((local_experts * hidden, width), jnp.bfloat16),
+            pltpu.VMEM((everyone // 2, local_experts * hidden), jnp.bfloat16),
             pltpu.SemaphoreType.DMA((3 * local_experts,)),
             pltpu.SemaphoreType.DMA((9, depth)),
             pltpu.SemaphoreType.DMA((9, depth)),
-            pltpu.SemaphoreType.DMA((4, max(depth, 2))),
-            pltpu.SemaphoreType.DMA((4, max(depth, 2))),
+            pltpu.SemaphoreType.DMA((8, max(depth, 2))),
+            pltpu.SemaphoreType.DMA((8, max(depth, 2))),
         ],
         compiler_params=pltpu.CompilerParams(
             collective_id=0, has_side_effects=True, vmem_limit_bytes=56 << 20
@@ -329,7 +354,7 @@
         cost_estimate=pl.CostEstimate(
             flops=6 * everyone * weights, bytes_accessed=6 * weights, transcendentals=0
         ),
-    )(tokens, expert_ids, gate_weights, live_counts, w_gate, w_up, w_down)
+    )(tokens, expert_ids.T, gate_weights.T, live_counts, w_gate, w_up, w_down)
 
 
 def body(tokens, expert_ids, gate_weights, live_counts, w_gate, w_up, w_down):

time: 72 us -> 65.7 us (0.913)
  Pallas kernels: 67.5 us -> 63.9 us
  local copies, waits for them, and re-layouts: 4.31 us -> 1.55 us
    pallas_call x1, Pallas kernels: 67.5 us -> 63.9 us  [fused_body(): pl.pallas_call(fused_kernel, out_shape=jax.ShapeDtypeStruct((rows, width)...]
    unnamed x3 -> x1, local copies, waits for them, and re-layouts: 4.31 us -> 1.55 us
where the time goes in v3:
time: 65.7 us; the launch traced here: 65.5 us
  Pallas kernels  63.9 us (97%)
  local copies, waits for them, and re-layouts  1.55 us (2%)
    pallas_call x1, Pallas kernels, fused_body(): pl.pallas_call(fused_kernel, out_shape=jax.ShapeDtypeStruct((rows, width)...  63.9 us
    unnamed x1, local copies, waits for them, and re-layouts  1.55 us

profile of v3, /device:TPU:0, one launch (start us, length us, event | category | flops | bytes accessed | tf_op | source)
XLA Modules:
  0.0 65.5 jit_solution(8416767871360377370)
XLA Ops:
  0.0 63.9 %shard_map.73 = bf16[16,3584]{1,0:T(8,128)(2,1)} custom-call(bf16[16,3584]{1,0:T(8,128)(2,1)} %tokens_ref.1, s32[8,64]{1,0:T(8,128)} %bitcast.2, f32[8,64]{1,0:T(8,128)} %bitcast.3, s32[4]{0:T(128)} %counts_ref.1, bf16[2,3584,256]{2,1,0:T(8,128)(2,1)} %gate_hbm.1, bf16[2,3584,256]{2,1,0:T(8,128)(2,1)} %up_hbm.1, bf16[2,256,3584]{2,1,0:T(8,128)(2,1)} %down_hbm.1), custom_call_target="tpu_custom_call" | custom-call | flops 5637144576 | bytes 11010048 | tf_op jit(solution)/shard_map/pallas_call | solution.py:329
  63.9 1.6 %copy.9 = bf16[16,3584]{1,0:T(8,128)(2,1)} copy(bf16[16,3584]{1,0:T(8,128)(2,1)} %shard_map.73) | data formatting | bytes 229376

commit v4 on v3

--- a/solution.py
+++ b/solution.py
@@ -110,7 +110,9 @@
     y_peer, x_peer = device(z, 1 - y, x, c), device(z, y, 1 - x, c)
     core_peer = device(z, y, x, 1 - c)
     hops = [(z + k) % depth for k in range(depth)]
-    came = [(z + depth - k) % depth for k in range(depth)]
+    nearest = [sorted(range(depth), key=lambda o, v=v: (abs(o - v), o)) for v in range(depth)]
+    came = [sum(jnp.where(z == v, nearest[v][k], 0) for v in range(depth)) for k in range(depth)]
+    above, below = device(z + 1, y, x, c), device(z - 1, y, x, c)
     line = [device(hops[k], y, x, c) for k in range(1, depth)]
 
     mine = pl.ds(place(c, y, x, z), rows)
@@ -157,12 +159,23 @@
         sent.append(copy)
 
     start_own = place(c, y, x, z)
-    for k in range(1, depth):
-        send(0, k, start_own, 0, full, line[k - 1])
+    own_piece = table.at[pl.ds(start_own, rows), :]
+    own_above = remote(own_piece, own_piece, gs.at[0, z], gr.at[0, z], above)
+    own_below = remote(own_piece, own_piece, gs.at[9, z], gr.at[0, z], below)
+    chain = [(z + 1 < depth, own_above), (z > 0, own_below)]
+    pl.when(z + 1 < depth)(own_above.start)
+    pl.when(z > 0)(own_below.start)
     for k in range(depth):
         here = place(c, y, x, came[k])
         if k > 0:
-            spread(0, k, here, 0, full, core_peer).wait_recv()
+            source = came[k]
+            spread(0, source, here, 0, full, above).wait_recv()
+            rising = source < z
+            onward = jnp.where(rising, z + 1, z - 1)
+            passes = (onward >= 0) & (onward < depth)
+            relay = spread(0, source, here, 0, full, device(onward, y, x, c))
+            pl.when(passes)(relay.start)
+            chain.append((passes, relay))
         send(1, k, here, 0, full, y_peer)
         send(2, k, here, 0, full, x_peer)
         send(5, k, here, 0, full, core_peer)
@@ -317,6 +330,8 @@
 
     for copy in sent:
         copy.wait_send()
+    for done, copy in chain:
+        pl.when(done)(copy.wait_send)
 
 
 def fused_body(tokens, expert_ids, gate_weights, live_counts, w_gate, w_up, w_down):
@@ -343,8 +358,8 @@
             pltpu.VMEM((local_experts * hidden, width), jnp.bfloat16),
             pltpu.VMEM((everyone // 2, local_experts * hidden), jnp.bfloat16),
             pltpu.SemaphoreType.DMA((3 * local_experts,)),
-            pltpu.SemaphoreType.DMA((9, depth)),
-            pltpu.SemaphoreType.DMA((9, depth)),
+            pltpu.SemaphoreType.DMA((10, depth)),
+            pltpu.SemaphoreType.DMA((10, depth)),
             pltpu.SemaphoreType.DMA((8, max(depth, 2))),
             pltpu.SemaphoreType.DMA((8, max(depth, 2))),
         ],

time: 65.7 us -> 62.4 us (0.950)
  Pallas kernels: 63.9 us -> 60.7 us
    pallas_call x1, Pallas kernels: 63.9 us -> 60.7 us  [fused_body(): pl.pallas_call(fused_kernel, out_shape=jax.ShapeDtypeStruct((rows, width)...]
where the time goes in v4:
time: 62.4 us; the launch traced here: 62.3 us
  Pallas kernels  60.7 us (97%)
  local copies, waits for them, and re-layouts  1.55 us (2%)
    pallas_call x1, Pallas kernels, fused_body(): pl.pallas_call(fused_kernel, out_shape=jax.ShapeDtypeStruct((rows, width)...  60.7 us
    unnamed x1, local copies, waits for them, and re-layouts  1.55 us

profile of v4, /device:TPU:0, one launch (start us, length us, event | category | flops | bytes accessed | tf_op | source)
XLA Modules:
  0.0 62.3 jit_solution(16444161971487252111)
XLA Ops:
  0.0 60.7 %shard_map.73 = bf16[16,3584]{1,0:T(8,128)(2,1)} custom-call(bf16[16,3584]{1,0:T(8,128)(2,1)} %tokens_ref.1, s32[8,64]{1,0:T(8,128)} %bitcast.2, f32[8,64]{1,0:T(8,128)} %bitcast.3, s32[4]{0:T(128)} %counts_ref.1, bf16[2,3584,256]{2,1,0:T(8,128)(2,1)} %gate_hbm.1, bf16[2,3584,256]{2,1,0:T(8,128)(2,1)} %up_hbm.1, bf16[2,256,3584]{2,1,0:T(8,128)(2,1)} %down_hbm.1), custom_call_target="tpu_custom_call" | custom-call | flops 5637144576 | bytes 11010048 | tf_op jit(solution)/shard_map/pallas_call | solution.py:344
  60.7 1.6 %copy.9 = bf16[16,3584]{1,0:T(8,128)(2,1)} copy(bf16[16,3584]{1,0:T(8,128)(2,1)} %shard_map.73) | data formatting | bytes 229376

commit v5 on v4

--- a/solution.py
+++ b/solution.py
@@ -221,8 +221,10 @@
     def spot(k):
         return pl.ds(pl.multiple_of(hops[k] * rows, rows), rows)
 
+    cut = (width // LANES * 3 // 4) * LANES
+
     def corner(side, k):
-        lo, hi = (0, half) if side == 0 else (half, width)
+        lo, hi = (0, cut) if side == 0 else (cut, width)
         piece = partial.at[slot(1 - y, 1 - x, k), lo:hi]
         landing = from_diag.at[spot(k), lo:hi]
         peer = x_peer if side == 0 else y_peer
@@ -230,7 +232,7 @@
 
     def side_copy(kind, k):
         py, px, peer, side = (y, 1 - x, x_peer, 1) if kind < 5 else (1 - y, x, y_peer, 0)
-        lo, hi = (0, half) if kind in (3, 6) else (half, width)
+        lo, hi = (0, cut) if kind in (3, 6) else (cut, width)
         piece = partial.at[slot(py, px, k), lo:hi]
         landing = from_side.at[side, spot(k), lo:hi]
         return remote(piece, landing, rs.at[kind, k], rr.at[kind, k], peer)
@@ -302,7 +304,7 @@
     for k in order:
         for side, kind, py, px in ((0, 6, 1 - y, x), (1, 4, y, 1 - x)):
             corner(side, k).wait_recv()
-            lo, hi = (0, half) if side == 0 else (half, width)
+            lo, hi = (0, cut) if side == 0 else (cut, width)
             here, there = slot(py, px, k), spot(k)
             total = partial[here, lo:hi].astype(jnp.float32) + from_diag[there, lo:hi].astype(jnp.float32)
             partial[here, lo:hi] = total.astype(jnp.bfloat16)

time: 62.4 us -> 59.9 us (0.960)
  Pallas kernels: 60.7 us -> 58.2 us
    pallas_call x1, Pallas kernels: 60.7 us -> 58.2 us  [fused_body(): pl.pallas_call(fused_kernel, out_shape=jax.ShapeDtypeStruct((rows, width)...]
where the time goes in v5:
time: 59.9 us; the launch traced here: 59.7 us
  Pallas kernels  58.2 us (97%)
  local copies, waits for them, and re-layouts  1.55 us (3%)
    pallas_call x1, Pallas kernels, fused_body(): pl.pallas_call(fused_kernel, out_shape=jax.ShapeDtypeStruct((rows, width)...  58.2 us
    unnamed x1, local copies, waits for them, and re-layouts  1.55 us

profile of v5, /device:TPU:0, one launch (start us, length us, event | category | flops | bytes accessed | tf_op | source)
XLA Modules:
  0.0 59.7 jit_solution(5485125755069568728)
XLA Ops:
  0.0 58.2 %shard_map.73 = bf16[16,3584]{1,0:T(8,128)(2,1)} custom-call(bf16[16,3584]{1,0:T(8,128)(2,1)} %tokens_ref.1, s32[8,64]{1,0:T(8,128)} %bitcast.2, f32[8,64]{1,0:T(8,128)} %bitcast.3, s32[4]{0:T(128)} %counts_ref.1, bf16[2,3584,256]{2,1,0:T(8,128)(2,1)} %gate_hbm.1, bf16[2,3584,256]{2,1,0:T(8,128)(2,1)} %up_hbm.1, bf16[2,256,3584]{2,1,0:T(8,128)(2,1)} %down_hbm.1), custom_call_target="tpu_custom_call" | custom-call | flops 5637144576 | bytes 11010048 | tf_op jit(solution)/shard_map/pallas_call | solution.py:346
  58.2 1.6 %copy.9 = bf16[16,3584]{1,0:T(8,128)(2,1)} copy(bf16[16,3584]{1,0:T(8,128)(2,1)} %shard_map.73) | data formatting | bytes 229376

commit v6 on v5

--- a/solution.py
+++ b/solution.py
@@ -176,9 +176,11 @@
             relay = spread(0, source, here, 0, full, device(onward, y, x, c))
             pl.when(passes)(relay.start)
             chain.append((passes, relay))
+        send(2, k, here, 0, full, x_peer)
         send(1, k, here, 0, full, y_peer)
-        send(2, k, here, 0, full, x_peer)
-        send(5, k, here, 0, full, core_peer)
+        if k > 0:
+            send(5, k - 1, place(c, y, x, came[k - 1]), 0, full, core_peer)
+    send(5, depth - 1, place(c, y, x, came[depth - 1]), 0, full, core_peer)
     for k in range(depth):
         here = place(c, 1 - y, x, came[k])
         spread(1, k, here, 0, full, y_peer).wait_recv()
@@ -251,7 +253,7 @@
         for k in order:
             add_core(y, x, k)
 
-    def compute(i, py, between, before_down):
+    def compute(i, py, between, before_down, after_send=lambda: None):
         start = place(0, py, 0, 0)
         span = pl.ds(start, 2 * chunk)
         extra = table[span, width:full].astype(jnp.float32)
@@ -279,6 +281,7 @@
 
             if core is not c:
                 emit(across(i, py))
+                after_send()
 
     def nothing():
         pass
@@ -287,7 +290,7 @@
         load.wait()
     meet(5, y, x)
     meet(7, y, 1 - x)
-    compute(0, y, nothing, finish_gather)
+    compute(0, y, nothing, nothing, finish_gather)
     meet(6, 1 - y, x)
     meet(8, 1 - y, 1 - x)
     compute(1, 1 - y, early, nothing)

time: 59.9 us -> 59.6 us (level)
  no operation moved by 1% of the time
where the time goes in v6:
time: 59.6 us; the launch traced here: 59.5 us
  Pallas kernels  57.9 us (97%)
  local copies, waits for them, and re-layouts  1.55 us (3%)
    pallas_call x1, Pallas kernels, fused_body(): pl.pallas_call(fused_kernel, out_shape=jax.ShapeDtypeStruct((rows, width)...  57.9 us
    unnamed x1, local copies, waits for them, and re-layouts  1.55 us

profile of v6, /device:TPU:0, one launch (start us, length us, event | category | flops | bytes accessed | tf_op | source)
XLA Modules:
  0.0 59.5 jit_solution(16837996061136451033)
XLA Ops:
  0.0 57.9 %shard_map.73 = bf16[16,3584]{1,0:T(8,128)(2,1)} custom-call(bf16[16,3584]{1,0:T(8,128)(2,1)} %tokens_ref.1, s32[8,64]{1,0:T(8,128)} %bitcast.2, f32[8,64]{1,0:T(8,128)} %bitcast.3, s32[4]{0:T(128)} %counts_ref.1, bf16[2,3584,256]{2,1,0:T(8,128)(2,1)} %gate_hbm.1, bf16[2,3584,256]{2,1,0:T(8,128)(2,1)} %up_hbm.1, bf16[2,256,3584]{2,1,0:T(8,128)(2,1)} %down_hbm.1), custom_call_target="tpu_custom_call" | custom-call | flops 5637144576 | bytes 11010048 | tf_op jit(solution)/shard_map/pallas_call | solution.py:349
  57.9 1.6 %copy.9 = bf16[16,3584]{1,0:T(8,128)(2,1)} copy(bf16[16,3584]{1,0:T(8,128)(2,1)} %shard_map.73) | data formatting | bytes 229376
